TPU v7x, 512 devices: a whole 4x4x16 slice. The times are simulated.
512 devices in a mesh: dp: 128 (over z, y, core), mp: 4 (over x).
Axes of the slice: x: 4, y: 4, z: 16, core: 2. Of those that a mesh axis runs over, the one named last changes fastest.
Arguments:
- covariates: bfloat16 [262144, 512], P('dp', 'mp'), may hold values from -6 to 6
- weight: float32 [512, 256], P(None, 'mp'), may hold values from -0.25 to 0.25
- scale: float32 [4, 256], P(None, 'mp'), may hold values from 0.3 to 1.5
- z_lane: float32 [8192, 256], P('dp', 'mp'), may hold values from -6 to 6
- z_supplier: float32 [4096, 256], P('dp', 'mp'), may hold values from -6 to 6
- z_region: float32 [64, 256], P(None, 'mp'), may hold values from -6 to 6
- z_company: float32 [8, 256], P(None, 'mp'), may hold values from -6 to 6
- group_owner: int32 [8192, 1], P('dp'), may hold values from 0 to 127; in each aligned block of 64 rows (0 to 63, 64 to 127, ...) at most 2 rows name the same one
- group_local: int32 [8192], P('dp'), may hold values from 0 to 63
- group_len: int32 [8192], P('dp'), may hold values from 1 to 32, 157286 in all
- event_bin: int32 [262144], P('dp'), may hold values from 0 to 255
- observed: int32 [262144], P('dp'), may hold values 0 or 1
- lane_supplier: int32 [8192], P('dp'), may hold values from 0 to 4095
- supplier_region: int32 [4096], replicated, may hold values from 0 to 63
- region_company: int32 [64], replicated, may hold values from 0 to 7
Outputs:
- grad_weight: float32 [512, 256], P(None, 'mp')
- grad_lane: float32 [8192, 256], P('dp', 'mp')
- grad_supplier: float32 [4096, 256], P('dp', 'mp')
- grad_region: float32 [64, 256], P(None, 'mp')
- grad_company: float32 [8, 256], P(None, 'mp')
- grad_scale: float32 [4, 256], P(None, 'mp')
Inputs may be any that keep to these rules, and one draw needn't show every extreme that they name: `group_owner`: among the 64 groups of one index of dp no owner is named more than 2 times, a bound that some block reaches.
All inputs are finite; a program needn't handle non-finite values. No bound on the sum of `group_len` or of `observed` on one device may be relied on, other than what follows from the above.
Results may differ from a plain program's by a relative error of at most 0.003.
Values may be sent and summed in bfloat16 or wider, within the bound.
A program may use at most 64 MiB of HBM per device.

v0:
```python
import jax
import jax.numpy as jnp
from jax import lax
from jax.sharding import PartitionSpec as P

HIGHEST = lax.Precision.HIGHEST


def select_rows(row_index, row_count, lookup):
    picks = (row_index[:, None] == jnp.arange(row_count, dtype=jnp.int32)[None, :]).astype(
        jnp.float32
    )
    return jnp.dot(picks, lookup, precision=HIGHEST)


def total_rows(row_index, row_count, values):
    picks = (row_index[:, None] == jnp.arange(row_count, dtype=jnp.int32)[None, :]).astype(
        jnp.float32
    )
    return lax.dot_general(picks, values, (((0,), (0,)), ((), ())), precision=HIGHEST)


def group_scores(covers, weight_cast, group_offset, bin_start, group_len, event_bin, observed):
    groups = group_len.shape[0]
    slot_count = covers.shape[0] // groups
    bin_width = weight_cast.shape[1]
    linear = jnp.dot(covers, weight_cast, preferred_element_type=jnp.float32)
    eta = (
        linear.reshape(groups, slot_count, bin_width) + group_offset.astype(jnp.float32)[:, None, :]
    )
    hazard = jax.nn.sigmoid(eta)
    bins = (bin_start + jnp.arange(bin_width, dtype=jnp.int32))[None, None, :]
    events = event_bin.reshape(groups, slot_count, 1)
    flags = observed.reshape(groups, slot_count, 1).astype(jnp.float32)
    live = (jnp.arange(slot_count, dtype=jnp.int32)[None, :] < group_len[:, None]).astype(
        jnp.float32
    )[:, :, None]
    score = live * jnp.where(
        bins < events, -hazard, jnp.where(bins == events, flags - hazard, jnp.float32(0.0))
    )
    score_rows = score.reshape(groups * slot_count, bin_width).astype(jnp.bfloat16)
    weight_part = lax.dot_general(
        covers, score_rows, (((0,), (0,)), ((), ())), preferred_element_type=jnp.float32
    )
    return (weight_part, jnp.sum(score, axis=1))


def per_device(
    covariates,
    weight,
    scale,
    z_lane,
    z_supplier,
    z_region,
    z_company,
    group_owner,
    group_local,
    group_len,
    event_bin,
    observed,
    lane_supplier,
    supplier_region,
    region_company,
):
    bin_width = weight.shape[1]
    groups = group_len.shape[0]
    owners = lax.axis_size("dp")
    lanes_dev = z_lane.shape[0]
    supplier_count = z_supplier.shape[0]
    regions = z_region.shape[0]
    companies = z_company.shape[0]
    device_index = lax.axis_index("dp")
    company_effect = scale[0] * z_company
    region_effect = scale[1] * z_region + select_rows(region_company, companies, company_effect)
    own_regions = lax.dynamic_slice_in_dim(
        supplier_region, device_index * supplier_count, supplier_count
    )
    path_own = scale[2] * z_supplier + select_rows(own_regions, regions, region_effect)
    all_paths, all_latent = (
        lax.all_gather(path_own, "dp", axis=0, tiled=True),
        lax.all_gather(z_supplier, "dp", axis=0, tiled=True),
    )
    supplier_all = all_paths.shape[0]
    lane_offset = (scale[3] * z_lane + jnp.take(all_paths, lane_supplier, axis=0)).astype(
        jnp.bfloat16
    )
    owner_id = group_owner[:, 0]
    capacity = max(2, 2 * groups // owners)
    marks = (owner_id[:, None] == jnp.arange(owners, dtype=jnp.int32)[None, :]).astype(jnp.int32)
    before = jnp.cumsum(marks, axis=0) - marks
    ranked = jnp.sum(before * marks, axis=1)
    slot_id = owner_id * capacity + ranked
    request = jnp.full((owners * capacity,), lanes_dev, jnp.int32).at[slot_id].set(group_local)
    request = request.reshape(owners, capacity)
    held = lax.all_to_all(request, "dp", split_axis=0, concat_axis=0, tiled=True)
    picks = (held[:, :, None] == jnp.arange(lanes_dev, dtype=jnp.int32)[None, None, :]).astype(
        jnp.bfloat16
    )
    found = jnp.einsum(
        "pkl,lb->pkb", picks, lane_offset, preferred_element_type=jnp.float32
    ).astype(jnp.bfloat16)
    replied = lax.all_to_all(found, "dp", split_axis=0, concat_axis=0, tiled=True)
    group_offset = jnp.take(replied.reshape(owners * capacity, bin_width), slot_id, axis=0)
    weight_cast = weight.astype(jnp.bfloat16)
    covers = lax.all_gather(covariates, "mp", axis=1, tiled=True)
    weight_part, group_sum = group_scores(
        covers,
        weight_cast,
        group_offset,
        lax.axis_index("mp") * bin_width,
        group_len,
        event_bin,
        observed,
    )
    outgoing = jnp.zeros((owners * capacity, bin_width), jnp.float32).at[slot_id].set(group_sum)
    incoming = lax.all_to_all(
        outgoing.reshape(owners, capacity, bin_width), "dp", split_axis=0, concat_axis=0, tiled=True
    )
    picks = (held[:, :, None] == jnp.arange(lanes_dev, dtype=jnp.int32)[None, None, :]).astype(
        jnp.float32
    )
    lane_total = jnp.einsum("pkl,pkb->lb", picks, incoming, precision=HIGHEST)
    supplier_part = (
        jnp.zeros((supplier_all, bin_width), jnp.float32).at[lane_supplier].add(lane_total)
    )
    scale_part = jnp.stack(
        [
            jnp.sum(jnp.take(all_latent, lane_supplier, axis=0) * lane_total, axis=0),
            jnp.sum(z_lane * lane_total, axis=0),
        ]
    )
    supplier_sum, weight_sum, scale_sum = lax.psum((supplier_part, weight_part, scale_part), "dp")
    region_total = total_rows(supplier_region, regions, supplier_sum)
    supplier_own = lax.dynamic_slice_in_dim(
        supplier_sum, device_index * supplier_count, supplier_count, 0
    )
    company_total = total_rows(region_company, companies, region_total)
    grad_scale = jnp.stack(
        [
            jnp.sum(z_company * company_total, axis=0),
            jnp.sum(z_region * region_total, axis=0),
            scale_sum[0],
            scale_sum[1],
        ]
    )
    return (
        weight_sum - weight,
        scale[3] * lane_total - z_lane,
        scale[2] * supplier_own - z_supplier,
        scale[1] * region_total - z_region,
        scale[0] * company_total - z_company,
        grad_scale,
    )


def solution(mesh):
    in_specs = (
        P("dp", "mp"),
        P(None, "mp"),
        P(None, "mp"),
        P("dp", "mp"),
        P("dp", "mp"),
        P(None, "mp"),
        P(None, "mp"),
        P("dp", None),
        P("dp"),
        P("dp"),
        P("dp"),
        P("dp"),
        P("dp"),
        P(),
        P(),
    )
    out_specs = (
        P(None, "mp"),
        P("dp", "mp"),
        P("dp", "mp"),
        P(None, "mp"),
        P(None, "mp"),
        P(None, "mp"),
    )
    return jax.shard_map(
        per_device, mesh=mesh, in_specs=in_specs, out_specs=out_specs, check_vma=False
    )
```

profile of v0, /device:TPU:1, one launch (start us, length us, event | category | flops | bytes accessed | tf_op | source)
XLA Modules:
  0.0 735.6 jit_solution(11509734262748519269)
XLA Ops:
  7.2 0.8 slice_bitcast_fusion.3
  8.8 1.0 convolution_add_fusion
  9.8 1.5 convolution_add_fusion.1
  13.7 0.8 select_reduce_fusion
  15.2 0.9 scatter_custom_fusion
  16.1 0.8 all_to_all.12
  16.9 20.7 %all-to-all-start = ((s32[128,1,2]{2,1,0:T(1,128)}), s32[128,1,2]{2,1,0:T(1,128)S(1)}, u32[]{:S(2)}, u32[]{:S(2)}) async-start(s32[128,1,2]{2,1,0:T(1,128)} %bitcast.4), calls=%async_computation | async-start | bytes 131072 | tf_op jit(solution)/shard_map/all_to_all | solution.py:95
  39.6 12.8 %all-to-all-done = s32[128,1,2]{2,1,0:T(1,128)S(1)} async-done(((s32[128,1,2]{2,1,0:T(1,128)}), s32[128,1,2]{2,1,0:T(1,128)S(1)}, u32[]{:S(2)}, u32[]{:S(2)}) %all-to-all-start) | async-done | bytes 1056 | tf_op jit(solution)/shard_map/all_to_all | solution.py:95
  52.5 104.9 %all-gather.6.cloned.1.call-done = f32[4096,64]{1,0:T(8,128)} async-done(((f32[32,64]{1,0:T(8,128)}), f32[4096,64]{1,0:T(8,128)}) %all-gather.6.cloned.1.call-update) | async-done | bytes 1048592 | tf_op jit(solution)/shard_map/all_gather | solution.py:80
  157.4 2.2 gather_fusion.1
  159.6 1.0 convolution_convert_fusion
  161.4 11.1 %all-to-all-start.1 = ((bf16[128,2,64]{2,1,0:T(2,128)(2,1)}), bf16[128,2,64]{2,1,0:T(2,128)(2,1)S(1)}, u32[]{:S(2)}, u32[]{:S(2)}) async-start(bf16[128,2,64]{2,1,0:T(2,128)(2,1)} %copy.32), calls=%async_computation.1 | async-start | bytes 131072 | tf_op jit(solution)/shard_map/all_to_all | solution.py:102
  173.4 0.8 lt.78
  174.2 122.5 %all-gather.8.cloned.1.call-done = f32[4096,64]{1,0:T(8,128)} async-done(((f32[32,64]{1,0:T(8,128)}), f32[4096,64]{1,0:T(8,128)}) %all-gather.8.cloned.1.call-update) | async-done | bytes 1048592 | tf_op jit(solution)/shard_map/all_gather | solution.py:81
  296.7 2.2 gather_fusion.2
  299.6 1.1 copy.33
  300.8 35.1 %all-gather.4.cloned.1.call-done = bf16[2048,512]{1,0:T(8,128)(2,1)} async-done(((bf16[2048,128]{1,0:T(8,128)(2,1)}), bf16[2048,512]{1,0:T(8,128)(2,1)}) %all-gather.4.cloned.1.call-update) | async-done | bytes 2097168 | tf_op jit(solution)/shard_map/all_gather | solution.py:105
  335.8 3.1 fusion.13
  339.0 1.5 copy.34
  340.5 1.0 multiply_reduce_fusion
  341.5 0.8 scatter_custom_fusion.1
  343.0 17.5 %all-to-all-start.2 = ((f32[128,1,128]{2,1,0:T(1,128)}), f32[128,1,128]{2,1,0:T(1,128)S(1)}, u32[]{:S(2)}, u32[]{:S(2)}) async-start(f32[128,1,128]{2,1,0:T(1,128)} %reshape.175), calls=%async_computation.2 | async-start | bytes 131072 | tf_op jit(solution)/shard_map/all_to_all | solution.py:116
  360.6 2.4 convolution_bitcast_fusion
  363.0 12.5 %all-to-all-done.2 = f32[128,1,128]{2,1,0:T(1,128)S(1)} async-done(((f32[128,1,128]{2,1,0:T(1,128)}), f32[128,1,128]{2,1,0:T(1,128)S(1)}, u32[]{:S(2)}, u32[]{:S(2)}) %all-to-all-start.2) | async-done | bytes 65568 | tf_op jit(solution)/shard_map/all_to_all | solution.py:116
  376.0 0.8 reduce
  377.0 0.8 fusion.15
  377.8 2.2 scatter_custom_fusion.2
  380.0 246.7 %psum.23 = f32[2,64]{1,0:T(2,128)S(1)} all-reduce(f32[2,64]{1,0:T(2,128)S(1)} %pad_maximum_fusion.1), channel_id=1, replica_groups=mesh['dp'=128,'mp'=4] {'dp'}, use_global_device_ids=true, to_apply=%region_12.14 | all-reduce | flops 128 | bytes 1024 | tf_op jit(solution)/shard_map/psum | solution.py:132
  626.7 93.3 %all-reduce.3.cloned.1.call-done = (f32[512,64]{0,1:T(8,128)}, f32[4096,64]{1,0:T(8,128)}) async-done(((f32[512,64]{0,1:T(8,128)}, f32[4096,64]{1,0:T(8,128)}), (f32[512,64]{0,1:T(8,128)}, f32[4096,64]{1,0:T(8,128)})) %all-reduce.3.cloned.1.call-update) | async-done | bytes 1179664 | tf_op jit(solution)/shard_map/psum | solution.py:132
  720.0 1.4 multiply_subtract_fusion.2
  721.3 5.6 multiply_reduce_fusion.2
  727.6 0.9 multiply_reduce_fusion.3
  (53 shorter events, 11.1 us)
Async XLA Ops:
  7.2 150.3 %all-gather.6.cloned.1.call-start = ((), (), s32[]{:S(2)}) async-start(), calls=%async_computation.4 | async-start | bytes 2113536 | tf_op jit(solution)/shard_map/all_gather | solution.py:80
  11.4 285.3 %all-gather.8.cloned.1.call-start = ((), (), s32[]{:S(2)}) async-start(), calls=%async_computation.5 | async-start | bytes 2113536 | tf_op jit(solution)/shard_map/all_gather | solution.py:81
  12.1 323.7 %all-gather.4.cloned.1.call-start = ((), (), s32[]{:S(2)}) async-start(), calls=%async_computation.3 | async-start | bytes 2621440 | tf_op jit(solution)/shard_map/all_gather | solution.py:105
  16.9 319.0 %copy-start.1 = (f32[512,64]{0,1:T(8,128)S(1)}, f32[512,64]{0,1:T(8,128)}, u32[]{:S(2)}) copy-start(f32[512,64]{0,1:T(8,128)} %param.18) | copy-start | bytes 393220
  16.9 35.6 %all-to-all-start = ((s32[128,1,2]{2,1,0:T(1,128)}), s32[128,1,2]{2,1,0:T(1,128)S(1)}, u32[]{:S(2)}, u32[]{:S(2)}) async-start(s32[128,1,2]{2,1,0:T(1,128)} %bitcast.4), calls=%async_computation | async-start | bytes 131072 | tf_op jit(solution)/shard_map/all_to_all | solution.py:95
  161.4 137.4 %all-to-all-start.1 = ((bf16[128,2,64]{2,1,0:T(2,128)(2,1)}), bf16[128,2,64]{2,1,0:T(2,128)(2,1)S(1)}, u32[]{:S(2)}, u32[]{:S(2)}) async-start(bf16[128,2,64]{2,1,0:T(2,128)(2,1)} %copy.32), calls=%async_computation.1 | async-start | bytes 131072 | tf_op jit(solution)/shard_map/all_to_all | solution.py:102
  339.0 21.7 %copy-start = (bf16[2048,512]{1,0:T(8,128)(2,1)S(1)}, bf16[2048,512]{1,0:T(8,128)(2,1)}, u32[]{:S(2)}) copy-start(bf16[2048,512]{1,0:T(8,128)(2,1)} %all-gather.4.cloned.1.call-done) | copy-start | bytes 6291460
  339.0 21.7 %copy-start.7 = (s32[2048]{0:T(1024)S(1)}, s32[2048]{0:T(1024)}, u32[]{:S(2)}) copy-start(s32[2048]{0:T(1024)} %param.27) | copy-start | bytes 24580
  343.0 32.5 %all-to-all-start.2 = ((f32[128,1,128]{2,1,0:T(1,128)}), f32[128,1,128]{2,1,0:T(1,128)S(1)}, u32[]{:S(2)}, u32[]{:S(2)}) async-start(f32[128,1,128]{2,1,0:T(1,128)} %reshape.175), calls=%async_computation.2 | async-start | bytes 131072 | tf_op jit(solution)/shard_map/all_to_all | solution.py:116
  360.6 16.4 %copy-start.5 = (f32[64,64]{1,0:T(8,128)S(1)}, f32[64,64]{1,0:T(8,128)}, u32[]{:S(2)}) copy-start(f32[64,64]{1,0:T(8,128)} %param.20) | copy-start | bytes 49156
  360.6 359.4 %all-reduce.3.cloned.1.call-start = ((), (), s32[]{:S(2)}) async-start(), calls=%async_computation.6 | async-start | bytes 4456448 | tf_op jit(solution)/shard_map/psum | solution.py:132
  377.8 342.2 %copy-start.2 = (f32[32,64]{1,0:T(8,128)S(1)}, f32[32,64]{1,0:T(8,128)}, u32[]{:S(2)}) copy-start(f32[32,64]{1,0:T(8,128)} %param.21) | copy-start | bytes 24580
  377.8 343.6 %copy-start.3 = (f32[64,64]{1,0:T(8,128)S(1)}, f32[64,64]{1,0:T(8,128)}, u32[]{:S(2)}) copy-start(f32[64,64]{1,0:T(8,128)} %param.22) | copy-start | bytes 49156
  377.8 343.6 %copy-start.6 = (s32[4096]{0:T(1024)S(1)}, s32[4096]{0:T(1024)}, u32[]{:S(2)}) copy-start(s32[4096]{0:T(1024)} %param.30) | copy-start | bytes 49156
  380.0 347.7 %copy-start.8 = (f32[8,64]{1,0:T(8,128)S(1)}, f32[8,64]{1,0:T(8,128)}, u32[]{:S(2)}) copy-start(f32[8,64]{1,0:T(8,128)} %param.23) | copy-start | bytes 6148
  380.0 347.7 %copy-start.9 = (s32[64]{0:T(128)S(1)}, s32[64]{0:T(128)}, u32[]{:S(2)}) copy-start(s32[64]{0:T(128)} %param.31) | copy-start | bytes 772
  720.0 7.0 copy-start.4
Sparse Core Ops, SparseCore 0:
  11.7 145.6 all-gather.5
  160.6 136.0 all-gather.7
  298.8 37.0 all-gather.3
  380.1 339.8 all-reduce.2
where the time goes:
time: 737 us; the launch traced here: 736 us
  waiting for transfers between devices  382 us (52%)
  blocking collectives  247 us (34%)
  starting transfers between devices  49.5 us (7%)
  matrix products  16.3 us (2%)
  local copies, waits for them, and re-layouts  15 us (2%)
  between operations  14 us (2%)
  other arithmetic  11.8 us (2%)
    psum x1, blocking collectives, per_device(): lax.psum((supplier_part, weight_part, scale_part), 'dp')  247 us
    all_gather x1, waiting for transfers between devices, per_device(): lax.all_gather(z_supplier, 'dp', axis=0, tiled=True)  122 us
    all_gather x1, waiting for transfers between devices, per_device(): lax.all_gather(path_own, 'dp', axis=0, tiled=True)  105 us
    psum x1, waiting for transfers between devices, per_device(): lax.psum((supplier_part, weight_part, scale_part), 'dp')  93.3 us
    all_gather x1, waiting for transfers between devices, per_device(): covers = lax.all_gather(covariates, 'mp', axis=1, tiled=True)  35.1 us
    all_to_all x1, starting transfers between devices, per_device(): lax.all_to_all(request, 'dp', split_axis=0, concat_axis=0, tiled=True)  20.7 us
    all_to_all x1, starting transfers between devices, per_device(): lax.all_to_all(outgoing.reshape(owners, capacity, bin_width), 'dp', split...  17.5 us
  transfers between devices with their start and end apart: 7, of which 6 were waited for; matrix products, arithmetic and copies ran while one was open for 2% of the time, Pallas kernels for 0%

commit v1 on v0

v1 whole, which is shorter than its diff:
```python
import jax
import jax.numpy as jnp
from jax import lax
from jax.experimental import pallas as pl
from jax.experimental.pallas import tpu as pltpu
from jax.sharding import PartitionSpec as P

HIGHEST = lax.Precision.HIGHEST
F = jnp.float32
B = jnp.bfloat16
I = jnp.int32
CHUNKS = 4
ROWS = 2048
CH = ROWS // CHUNKS
HALF = CH // 2


def iota(shape, axis):
    return lax.broadcasted_iota(I, shape, axis)


def mm(a, b, ca=1, cb=0, precision=None):
    return lax.dot_general(
        a, b, (((ca,), (cb,)), ((), ())), preferred_element_type=F, precision=precision
    )


def pick(cond, dtype=F):
    return jnp.where(cond, jnp.float32(1.0), jnp.float32(0.0)).astype(dtype)


def column(row):
    n = row.shape[1]
    return jnp.sum(
        jnp.where(iota((n, n), 0) == iota((n, n), 1), row, jnp.zeros_like(row)),
        axis=1,
        keepdims=True,
    )


def row_of(col):
    n = col.shape[0]
    return jnp.sum(
        jnp.where(iota((n, n), 0) == iota((n, n), 1), col, jnp.zeros_like(col)),
        axis=0,
        keepdims=True,
    )


def side(a, b):
    return jnp.concatenate([a, b], axis=1)


def split(value):
    high = value.astype(B)
    low = (value - high.astype(F)).astype(B)
    return side(high, low)


def kernel(
    cov,
    weight,
    scale,
    z_lane,
    z_supplier,
    z_region,
    z_company,
    group_owner,
    group_local,
    group_len,
    event_bin,
    observed,
    lane_supplier,
    supplier_region,
    region_company,
    grad_weight,
    grad_lane,
    grad_supplier,
    grad_region,
    grad_company,
    grad_scale,
    covers,
    linear,
    scores,
    nodes,
    lane_ids,
    group_ids,
    found_ids,
    row_ids,
    reply,
    replied,
    sums,
    parts,
    parted,
    part_in,
    far_in,
    near_in,
    near_lane,
    whole,
    local_sem,
    send_sem,
    recv_sem,
):
    dp = lax.axis_index("dp")
    mp = lax.axis_index("mp")
    z = lax.div(dp, 8)
    yc = lax.rem(dp, 8)
    r = lax.rem(z, 4)
    q = lax.div(z, 4)
    right = lax.rem(mp + 1, 4)
    left = lax.rem(mp + 3, 4)

    def at_z(step):
        return {"dp": lax.rem(z + step, 16) * 8 + yc, "mp": mp}

    def at_yc(step):
        return {"dp": z * 8 + lax.rem(yc + step, 8), "mp": mp}

    def at_x(index):
        return {"dp": dp, "mp": index}

    count = [0]
    started = []

    def send(src, dst, device):
        slot = count[0]
        count[0] = slot + 1
        copy = pltpu.make_async_remote_copy(
            src_ref=src,
            dst_ref=dst,
            send_sem=send_sem.at[slot],
            recv_sem=recv_sem.at[slot],
            device_id=device,
            device_id_type=pl.DeviceIdType.MESH,
        )
        copy.start()
        started.append(copy)
        return copy

    def arrive(copies):
        for copy in copies:
            copy.wait_recv()

    def far(buf):
        return [send(buf.at[r, q], buf.at[r, q], at_z(step)) for step in (4, 12, 8)]

    def near(buf):
        return [
            send(buf.at[r], buf.at[r], at_z(1)),
            send(buf.at[r], buf.at[r], at_z(15)),
            send(buf.at[r, pl.ds(0, 2)], buf.at[r, pl.ds(0, 2)], at_z(2)),
            send(buf.at[r, pl.ds(2, 2)], buf.at[r, pl.ds(2, 2)], at_z(14)),
        ]

    def plane(buf):
        return [send(buf.at[yc], buf.at[yc], at_yc(step)) for step in range(1, 8)]

    def scatter(source, target):
        return [
            send(source.at[lax.rem(yc + step, 8)], target.at[yc], at_yc(step))
            for step in range(1, 8)
        ]

    barrier = pltpu.get_barrier_semaphore()
    partners = [at_yc(step) for step in range(1, 8)]
    partners += [at_z(step) for step in (1, 2, 4, 8, 12, 14, 15)]
    partners += [at_x(right), at_x(left)]
    for device in partners:
        pl.semaphore_signal(
            barrier, inc=1, device_id=device, device_id_type=pl.DeviceIdType.MESH
        )

    own_owner = row_of(group_owner[...].astype(F))
    own_local = group_local[...].astype(F)
    nodes[r, q, 0:64, :] = split(z_lane[...])
    nodes[r, q, 64:96, :] = split(z_supplier[...])
    lane_ids[r, q] = side(lane_supplier[...].astype(F), jnp.zeros((1, 64), F))
    group_ids[yc] = side(own_owner, own_local)
    pl.semaphore_wait(barrier, len(partners))

    chunk_rows = [pl.ds(c * CH, CH) for c in range(CHUNKS)]
    own_copies = []
    for c in range(CHUNKS):
        copy = pltpu.make_async_copy(
            cov.at[chunk_rows[c]], covers.at[mp, chunk_rows[c]], local_sem.at[c]
        )
        copy.start()
        own_copies.append(copy)
    group_id_copies = plane(group_ids)
    lane_id_copies = far(lane_ids)
    node_copies = far(nodes)
    direct = []
    for c in range(CHUNKS):
        block = covers.at[mp, chunk_rows[c]]
        direct.append(
            [
                send(cov.at[chunk_rows[c]], block, at_x(right)),
                send(cov.at[chunk_rows[c]], block, at_x(left)),
            ]
        )
    passed = []

    def forward(c):
        arrive(direct[c])
        first = covers.at[left, pl.ds(c * CH, HALF)]
        second = covers.at[right, pl.ds(c * CH + HALF, HALF)]
        passed.append([send(first, first, at_x(right)), send(second, second, at_x(left))])

    weight_rows = weight[...].T.astype(B)
    company_effect = scale[0:1, :] * z_company[...]
    companies = region_company[...]
    company_pick = pick(iota((64, 8), 1) == column(companies.astype(F)).astype(I))
    region_effect = scale[1:2, :] * z_region[...] + mm(
        company_pick, company_effect, precision=HIGHEST
    )
    lens = group_len[...].astype(F)
    spread = jnp.where(
        (iota((16, 64), 1) >> 2) == iota((16, 64), 0), lens, jnp.zeros_like(lens)
    )
    lanes_of = pick((iota((64, 128), 0) & 3) == (iota((64, 128), 1) >> 5), B)
    live_len = mm(spread.astype(B), lanes_of).astype(I)
    ends = jnp.where((iota((16, 128), 1) & 31) < live_len, event_bin[...], -1)
    flags = observed[...].astype(F)

    arrive(lane_id_copies)
    lane_id_copies = near(lane_ids)
    arrive(node_copies)
    node_copies = near(nodes)
    forward(0)

    arrive(group_id_copies)
    ids = jnp.concatenate([group_ids[j] for j in range(8)], axis=0).astype(I)
    owners, locals_ = ids[:, 0:64], ids[:, 64:128]
    owner_z = owners >> 3
    held = jnp.where((owners & 7) == yc, (owner_z & 3) * 4 + (owner_z >> 2), -1)
    lane_key = jnp.where(held >= 0, held * 64 + locals_, -1)

    arrive(lane_id_copies)
    table = jnp.concatenate([lane_ids[a, b] for a in range(4) for b in range(4)], axis=0)
    table = table.T[0:64, :]
    found = []
    for j in range(8):
        of_owner = mm(table, pick(iota((16, 64), 0) == held[j : j + 1, :]), precision=HIGHEST)
        found.append(
            jnp.sum(
                jnp.where(
                    iota((64, 64), 0) == locals_[j : j + 1, :], of_owner, jnp.float32(0.0)
                ),
                axis=0,
                keepdims=True,
            )
        )
    found = jnp.concatenate(found, axis=0)
    found_ids[yc] = side(found, jnp.zeros((8, 64), F))
    found_copies = plane(found_ids)
    forward(1)

    lane_columns = [
        column(lane_key[j : j + 1, :].astype(F)).astype(I) for j in range(8)
    ]

    arrive(found_copies)
    suppliers = found_ids[0]
    for j in range(1, 8):
        suppliers = suppliers + found_ids[j]
    suppliers = suppliers[:, 0:64]
    own_supplier = jnp.sum(
        jnp.where(iota((8, 64), 0) == yc, suppliers, jnp.float32(0.0)), axis=0, keepdims=True
    )
    row_ids[r, q] = side(own_supplier, own_owner * 64.0 + own_local)
    row_id_copies = far(row_ids)
    suppliers = suppliers.astype(I)
    sup_owner = suppliers >> 5
    sup_z = sup_owner >> 3
    sup_key = jnp.where(
        (sup_owner & 7) == yc,
        ((sup_z & 3) * 4 + (sup_z >> 2)) * 32 + (suppliers & 31),
        -1,
    )
    forward(2)

    own_sup_col = column(own_supplier).astype(I)
    sup_row = pick(iota((64, 32), 1) == (own_sup_col >> 7), B)
    region_table = mm(sup_row, supplier_region[...].astype(F).astype(B))
    group_region = jnp.sum(
        jnp.where(iota((64, 128), 1) == (own_sup_col & 127), region_table, jnp.float32(0.0)),
        axis=1,
        keepdims=True,
    )
    region_col = group_region.astype(I)
    region_row = row_of(group_region).astype(I)
    group_effect = mm(
        pick(iota((64, 64), 1) == region_col), region_effect, precision=HIGHEST
    )
    arrive(row_id_copies)
    row_id_copies = near(row_ids)

    arrive(node_copies)
    lane_nodes = nodes[:, :, 0:64, :].reshape(1024, 128)
    sup_nodes = nodes[:, :, 64:96, :].reshape(512, 128)
    for j in range(8):
        lane_pick = pick(iota((64, 1024), 1) == lane_columns[j], B)
        sup_col = column(sup_key[j : j + 1, :].astype(F)).astype(I)
        sup_pick = pick(iota((64, 512), 1) == sup_col, B)
        reply[j, 0] = mm(lane_pick, lane_nodes).astype(B)
        reply[j, 1] = mm(sup_pick, sup_nodes).astype(B)
    replied[yc] = reply[yc]
    reply_copies = scatter(reply, replied)
    forward(3)

    arrive(row_id_copies)
    held_rows = jnp.concatenate(
        [row_ids[a, b] for a in range(4) for b in range(4)], axis=0
    ).astype(I)

    def along(start):
        return jnp.concatenate(
            [held_rows[k : k + 1, start : start + 32] for k in range(16)], axis=1
        )

    sup_along = side(along(0), along(32)) - z * 256
    lane_along = side(along(64), along(96)) - z * 512

    for c in range(CHUNKS):
        own_copies[c].wait()
        arrive(passed[c])
        rows = jnp.concatenate([covers[k, c * CH : (c + 1) * CH, :] for k in range(4)], axis=1)
        linear[:, c * CH : (c + 1) * CH] = mm(weight_rows, rows, 1, 1)

    arrive(reply_copies)
    got = replied[0].astype(F)
    for j in range(1, 8):
        got = got + replied[j].astype(F)
    lane_latent = got[0, :, 0:64] + got[0, :, 64:128]
    sup_latent = got[1, :, 0:64] + got[1, :, 64:128]
    path = scale[2:3, :] * sup_latent + group_effect
    offset = (scale[3:4, :] * lane_latent + path).astype(B)
    offset = offset.astype(F).T.astype(B)

    bins = iota((64, 128), 0) + mp * 64
    for s in range(16):
        at = slice(s * 128, (s + 1) * 128)
        expand = pick(iota((64, 128), 0) == (iota((64, 128), 1) >> 5) + 4 * s, B)
        eta = linear[:, at] + mm(offset, expand)
        hazard = jax.nn.sigmoid(eta)
        end = ends[s : s + 1, :]
        score = jnp.where(
            bins < end,
            -hazard,
            jnp.where(bins == end, flags[s : s + 1, :] - hazard, jnp.float32(0.0)),
        )
        scores[:, at] = score.astype(B)

    score_rows = scores[...]
    group_pick = pick(iota((64, 2048), 0) == (iota((64, 2048), 1) >> 5), B)
    group_sum = mm(group_pick, score_rows, 1, 1)
    sums[r, q] = side(group_sum[0:32, :], group_sum[32:64, :]).astype(B)
    sum_copies = far(sums)

    for pair in range(2):
        block = side(covers[2 * pair], covers[2 * pair + 1])
        product = mm(score_rows, block)
        for half in range(2):
            first = (2 * pair + half) * 64
            piece = product[:, half * 128 : (half + 1) * 128]
            done = 0
            while done < 64:
                where, inside = divmod(first + done, 40)
                size = min(40 - inside, 64 - done)
                parts[where, inside : inside + size, :] = piece[done : done + size, :]
                done += size
    by_region = mm(
        pick(iota((64, 64), 0) == region_row), group_sum, precision=HIGHEST
    )
    by_region = side(by_region[0:32, :], by_region[32:64, :])
    scale_part = side(
        jnp.sum(lane_latent * group_sum, axis=0, keepdims=True),
        jnp.sum(sup_latent * group_sum, axis=0, keepdims=True),
    )
    parts[6, 16:40, :] = by_region[0:24, :]
    parts[7, 0:8, :] = by_region[24:32, :]
    parts[7, 8:16, :] = jnp.where(iota((8, 128), 0) == 0, scale_part, jnp.float32(0.0))
    parts[7, 16:40, :] = jnp.zeros((24, 128), F)
    part_in[yc] = parts[yc]
    part_copies = scatter(parts, part_in)

    lane_hit = pick(iota((512, 1024), 0) == lane_along, B)
    sup_hit = pick(iota((256, 1024), 0) == sup_along, B)
    arrive(sum_copies)
    sum_copies = near(sums)
    arrive(part_copies)
    total = part_in[0]
    for j in range(1, 8):
        total = total + part_in[j]
    far_in[q] = total
    far_copies = [send(far_in.at[q], far_in.at[q], at_z(step)) for step in (4, 12, 8)]

    arrive(sum_copies)
    gathered = sums[...].reshape(512, 128)
    gathered = jnp.concatenate([gathered[:, 0:64], gathered[:, 64:128]], axis=0)
    by_lane = mm(lane_hit, gathered)
    by_supplier = mm(sup_hit, gathered)
    for j in range(8):
        parted[j, 0:32, :] = side(
            by_lane[j * 64 : j * 64 + 32, :], by_lane[j * 64 + 32 : j * 64 + 64, :]
        )
        parted[j, 32:48, :] = side(
            by_supplier[j * 32 : j * 32 + 16, :], by_supplier[j * 32 + 16 : j * 32 + 32, :]
        )
    near_lane[yc] = parted[yc]
    lane_copies = scatter(parted, near_lane)

    arrive(far_copies)
    near_in[r] = (far_in[0] + far_in[1]) + (far_in[2] + far_in[3])
    near_copies = [send(near_in.at[r], near_in.at[r], at_z(step)) for step in (1, 15, 2)]

    arrive(lane_copies)
    total = near_lane[0]
    for j in range(1, 8):
        total = total + near_lane[j]
    lane_total = jnp.concatenate([total[0:32, 0:64], total[0:32, 64:128]], axis=0)
    supplier_total = jnp.concatenate([total[32:48, 0:64], total[32:48, 64:128]], axis=0)
    grad_lane[...] = scale[3:4, :] * lane_total - z_lane[...]
    grad_supplier[...] = scale[2:3, :] * supplier_total - z_supplier[...]

    arrive(near_copies)
    whole[yc] = (near_in[0] + near_in[1]) + (near_in[2] + near_in[3])
    whole_copies = plane(whole)
    arrive(whole_copies)

    def whole_rows(first, size):
        pieces = []
        done = 0
        while done < size:
            where, inside = divmod(first + done, 40)
            step = min(40 - inside, size - done)
            pieces.append(whole[where, inside : inside + step, :])
            done += step
        return pieces[0] if len(pieces) == 1 else jnp.concatenate(pieces, axis=0)

    for k in range(4):
        at = slice(k * 128, (k + 1) * 128)
        grad_weight[at, :] = whole_rows(k * 64, 64).T - weight[at, :]
    by_region = whole_rows(256, 32)
    region_total = jnp.concatenate([by_region[:, 0:64], by_region[:, 64:128]], axis=0)
    scale_total = whole_rows(288, 8)[0:1, :]
    company_total = mm(
        pick(iota((8, 64), 0) == companies), region_total, precision=HIGHEST
    )
    grad_region[...] = scale[1:2, :] * region_total - z_region[...]
    grad_company[...] = scale[0:1, :] * company_total - z_company[...]
    grad_scale[0:1, :] = jnp.sum(z_company[...] * company_total, axis=0, keepdims=True)
    grad_scale[1:2, :] = jnp.sum(z_region[...] * region_total, axis=0, keepdims=True)
    grad_scale[2:3, :] = scale_total[:, 64:128]
    grad_scale[3:4, :] = scale_total[:, 0:64]

    for copy in started:
        copy.wait_send()


def per_device(
    covariates,
    weight,
    scale,
    z_lane,
    z_supplier,
    z_region,
    z_company,
    group_owner,
    group_local,
    group_len,
    event_bin,
    observed,
    lane_supplier,
    supplier_region,
    region_company,
):
    vmem = pl.BlockSpec(memory_space=pltpu.VMEM)
    slots = 160
    return pl.pallas_call(
        kernel,
        out_shape=(
            jax.ShapeDtypeStruct((512, 64), F),
            jax.ShapeDtypeStruct((64, 64), F),
            jax.ShapeDtypeStruct((32, 64), F),
            jax.ShapeDtypeStruct((64, 64), F),
            jax.ShapeDtypeStruct((8, 64), F),
            jax.ShapeDtypeStruct((4, 64), F),
        ),
        in_specs=[pl.BlockSpec(memory_space=pl.ANY)] + [vmem] * 14,
        out_specs=(vmem,) * 6,
        scratch_shapes=[
            pltpu.VMEM((4, ROWS, 128), B),
            pltpu.VMEM((64, ROWS), F),
            pltpu.VMEM((64, ROWS), B),
            pltpu.VMEM((4, 4, 96, 128), B),
            pltpu.VMEM((4, 4, 1, 128), F),
            pltpu.VMEM((8, 1, 128), F),
            pltpu.VMEM((8, 8, 128), F),
            pltpu.VMEM((4, 4, 1, 128), F),
            pltpu.VMEM((8, 2, 64, 128), B),
            pltpu.VMEM((8, 2, 64, 128), B),
            pltpu.VMEM((4, 4, 32, 128), B),
            pltpu.VMEM((8, 40, 128), F),
            pltpu.VMEM((8, 48, 128), F),
            pltpu.VMEM((8, 40, 128), F),
            pltpu.VMEM((4, 40, 128), F),
            pltpu.VMEM((4, 40, 128), F),
            pltpu.VMEM((8, 48, 128), F),
            pltpu.VMEM((8, 40, 128), F),
            pltpu.SemaphoreType.DMA((CHUNKS,)),
            pltpu.SemaphoreType.DMA((slots,)),
            pltpu.SemaphoreType.DMA((slots,)),
        ],
        compiler_params=pltpu.CompilerParams(
            collective_id=0, has_side_effects=True, vmem_limit_bytes=48 * 1024 * 1024
        ),
        name="hazard_gradient",
    )(
        covariates,
        weight,
        scale,
        z_lane,
        z_supplier,
        z_region,
        z_company,
        group_owner,
        group_local.reshape(1, 64),
        group_len.reshape(1, 64),
        event_bin.reshape(16, 128),
        observed.reshape(16, 128),
        lane_supplier.reshape(1, 64),
        supplier_region.reshape(32, 128),
        region_company.reshape(1, 64),
    )


def solution(mesh):
    in_specs = (
        P("dp", "mp"),
        P(None, "mp"),
        P(None, "mp"),
        P("dp", "mp"),
        P("dp", "mp"),
        P(None, "mp"),
        P(None, "mp"),
        P("dp", None),
        P("dp"),
        P("dp"),
        P("dp"),
        P("dp"),
        P("dp"),
        P(),
        P(),
    )
    out_specs = (
        P(None, "mp"),
        P("dp", "mp"),
        P("dp", "mp"),
        P(None, "mp"),
        P(None, "mp"),
        P(None, "mp"),
    )
    return jax.shard_map(
        per_device, mesh=mesh, in_specs=in_specs, out_specs=out_specs, check_vma=False
    )
```

time: 737 us -> 82.3 us (0.11)
  waiting for transfers between devices: 382 us -> 0 us
  blocking collectives: 247 us -> 0 us
  Pallas kernels: 0 us -> 74.5 us
  starting transfers between devices: 49.5 us -> 0 us
  matrix products: 16.3 us -> 0 us
  between operations: 14 us -> 0.85 us
  other arithmetic: 11.8 us -> 0 us
  local copies, waits for them, and re-layouts: 15 us -> 6.71 us
    all_gather x3 -> x0, waiting for transfers between devices: 262 us -> none  [the longest x1 122 us: per_device(): lax.all_gather(z_supplier, 'dp', axis=0, tiled=True)]
    psum x1 -> x0, blocking collectives: 247 us -> none  [per_device(): lax.psum((supplier_part, weight_part, scale_part), 'dp')]
    psum x1 -> x0, waiting for transfers between devices: 93.3 us -> none  [per_device(): lax.psum((supplier_part, weight_part, scale_part), 'dp')]
    pallas_call x0 -> x1, Pallas kernels: none -> 74.5 us  [per_device(): pl.pallas_call(kernel, out_shape=(jax.ShapeDtypeStruct((512, 64), F), jax...]
    all_to_all x3 -> x0, starting transfers between devices: 49.3 us -> none  [the longest x1 20.7 us: per_device(): lax.all_to_all(request, 'dp', split_axis=0, concat_axis=0, tiled=True)]
    all_to_all x3 -> x0, waiting for transfers between devices: 25.3 us -> none  [the longest x1 12.8 us: per_device(): lax.all_to_all(request, 'dp', split_axis=0, concat_axis=0, tiled=True)]
    dot_general x8 -> x0, matrix products: 16.3 us -> none  [the longest x2 6.47 us: total_rows(): lax.dot_general(picks, values, (((0,), (0,)), ((), ())), precision=HIGHEST)]
  transfers between devices with their start and end apart: 7 -> 0, of which waited for: 6 -> 0; matrix products, arithmetic and copies ran while one was open for 2% -> 0% of each run, Pallas kernels for 0% -> 0%
where the time goes in v1:
time: 82.3 us; the launch traced here: 82.1 us
  Pallas kernels  74.5 us (91%)
  local copies, waits for them, and re-layouts  6.71 us (8%)
  between operations  0.85 us (1%)
    pallas_call x1, Pallas kernels, per_device(): pl.pallas_call(kernel, out_shape=(jax.ShapeDtypeStruct((512, 64), F), jax...  74.5 us
    unnamed x35, local copies, waits for them, and re-layouts  5.94 us

profile of v1, /device:TPU:1, one launch (start us, length us, event | category | flops | bytes accessed | tf_op | source)
XLA Modules:
  0.0 82.1 jit_solution(4382537268255207422)
XLA Ops:
  0.6 0.0 copy-start.13
  0.6 0.6 copy-done.13
  1.3 0.1 copy.22.group_owner
  1.4 0.0 copy-start.3
  1.4 0.0 copy-start.4
  1.4 0.0 copy-start.5
  1.4 0.0 copy-start.6
  1.4 0.0 copy-start.7
  1.5 0.0 copy-start.8
  1.5 0.0 copy-start.9
  1.5 0.0 copy-start.10
  1.5 0.0 copy-start.11
  1.5 0.0 copy-start.12
  1.5 1.1 %copy.21.weight = f32[512,64]{1,0:T(8,128)S(1)} copy(f32[512,64]{0,1:T(8,128)} %param.16) | data formatting | bytes 262144 | tf_op args[1]
  2.6 0.0 copy-done.1
  2.6 0.0 copy-done.2
  2.6 0.0 copy-done.3
  2.6 0.0 copy-done.4
  2.6 0.0 copy-done.5
  2.7 0.0 copy-done.6
  2.7 0.0 copy-done.7
  2.7 0.0 copy-done.8
  2.7 0.0 copy-done.9
  2.7 0.0 copy-start
  2.7 1.0 %copy-done = bf16[2048,128]{1,0:T(8,128)(2,1)S(1)} copy-done((bf16[2048,128]{1,0:T(8,128)(2,1)S(1)}, bf16[2048,128]{1,0:T(8,128)(2,1)}, u32[]{:S(2)}) %copy-start) | copy-done | bytes 524312
  3.8 74.5 %hazard_gradient.1 = (f32[512,64]{1,0:T(8,128)S(1)}, f32[64,64]{1,0:T(8,128)S(1)}, f32[32,64]{1,0:T(8,128)S(1)}, f32[64,64]{1,0:T(8,128)S(1)}, f32[8,64]{1,0:T(8,128)S(1)}, /*index=5*/f32[4,64]{1,0:T(4,128)S(1)}) custom-call(bf16[2048,128]{1,0:T(8,128)(2,1)S(1)} %copy-done, f32[512,64]{1,0:T(8,128)S(1)} %copy.21.weight, f32[4,64]{1,0:T(4,128)S(1)} %copy-done.8, ...), custom_call_target="tpu_custom_call" | custom-call | tf_op jit(solution)/shard_map/hazard_gradient/pallas_call | solution.py:480
  78.3 0.8 copy.23
  79.1 0.6 copy.29
  79.7 0.6 copy.30
  80.3 0.6 copy.31
  80.9 0.6 copy.32
  81.5 0.6 copy.33
  (5 shorter events, 0.0 us)
Async XLA Ops:
  0.6 0.7 copy-start.13
  1.4 1.2 %copy-start.1 = (f32[64,64]{1,0:T(8,128)S(1)}, f32[64,64]{1,0:T(8,128)}, u32[]{:S(2)}) copy-start(f32[64,64]{1,0:T(8,128)} %z_lane.1) | copy-start | bytes 49156
  1.4 1.2 %copy-start.2 = (f32[64,64]{1,0:T(8,128)S(1)}, f32[64,64]{1,0:T(8,128)}, u32[]{:S(2)}) copy-start(f32[64,64]{1,0:T(8,128)} %z_region.1) | copy-start | bytes 49156
  1.4 1.2 %copy-start.3 = (f32[32,64]{1,0:T(8,128)S(1)}, f32[32,64]{1,0:T(8,128)}, u32[]{:S(2)}) copy-start(f32[32,64]{1,0:T(8,128)} %z_supplier.1) | copy-start | bytes 24580
  1.4 1.2 %copy-start.4 = (s32[4096]{0:T(1024)S(1)}, s32[4096]{0:T(1024)}, u32[]{:S(2)}) copy-start(s32[4096]{0:T(1024)} %param.28) | copy-start | bytes 49156
  1.4 1.2 %copy-start.5 = (s32[2048]{0:T(1024)S(1)}, s32[2048]{0:T(1024)}, u32[]{:S(2)}) copy-start(s32[2048]{0:T(1024)} %param.25) | copy-start | bytes 24580
  1.4 1.2 %copy-start.6 = (s32[2048]{0:T(1024)S(1)}, s32[2048]{0:T(1024)}, u32[]{:S(2)}) copy-start(s32[2048]{0:T(1024)} %param.26) | copy-start | bytes 24580
  1.4 1.2 %copy-start.7 = (f32[8,64]{1,0:T(8,128)S(1)}, f32[8,64]{1,0:T(8,128)}, u32[]{:S(2)}) copy-start(f32[8,64]{1,0:T(8,128)} %z_company.1) | copy-start | bytes 6148
  1.5 1.2 %copy-start.8 = (f32[4,64]{1,0:T(4,128)S(1)}, f32[4,64]{1,0:T(4,128)}, u32[]{:S(2)}) copy-start(f32[4,64]{1,0:T(4,128)} %scale.1) | copy-start | bytes 3076
  1.5 1.2 %copy-start.9 = (s32[64]{0:T(128)S(1)}, s32[64]{0:T(128)}, u32[]{:S(2)}) copy-start(s32[64]{0:T(128)} %param.23) | copy-start | bytes 772
  1.5 1.2 %copy-start.10 = (s32[64]{0:T(128)S(1)}, s32[64]{0:T(128)}, u32[]{:S(2)}) copy-start(s32[64]{0:T(128)} %param.24) | copy-start | bytes 772
  1.5 1.2 %copy-start.11 = (s32[64]{0:T(128)S(1)}, s32[64]{0:T(128)}, u32[]{:S(2)}) copy-start(s32[64]{0:T(128)} %param.27) | copy-start | bytes 772
  1.5 1.2 %copy-start.12 = (s32[64]{0:T(128)S(1)}, s32[64]{0:T(128)}, u32[]{:S(2)}) copy-start(s32[64]{0:T(128)} %param.29) | copy-start | bytes 772
  2.7 1.0 %copy-start = (bf16[2048,128]{1,0:T(8,128)(2,1)S(1)}, bf16[2048,128]{1,0:T(8,128)(2,1)}, u32[]{:S(2)}) copy-start(bf16[2048,128]{1,0:T(8,128)(2,1)} %cov.1) | copy-start | bytes 1572868

commit v2 on v0

v2 whole, which is shorter than its diff:
```python
import jax
import jax.numpy as jnp
from jax import lax
from jax.experimental import pallas as pl
from jax.experimental.pallas import tpu as pltpu
from jax.sharding import PartitionSpec as P

HIGHEST = lax.Precision.HIGHEST
F = jnp.float32
B = jnp.bfloat16
I = jnp.int32
S = jnp.int16
VMEM_BYTES = 60 * 1024 * 1024
CHUNKS = 8
ROWS = 2048
CH = ROWS // CHUNKS
HALF = CH // 2
STEPS = (8, 7, 9, 6, 10, 5, 11, 4, 12, 3, 13, 2, 14, 1, 15)
UNIT = 5461.0


def iota(shape, axis):
    return lax.broadcasted_iota(I, shape, axis)


def mm(a, b, ca=1, cb=0, precision=None):
    return lax.dot_general(
        a, b, (((ca,), (cb,)), ((), ())), preferred_element_type=F, precision=precision
    )


def pick(cond, dtype=F):
    return jnp.where(cond, jnp.float32(1.0), jnp.float32(0.0)).astype(dtype)


def column(row):
    n = row.shape[1]
    return jnp.sum(
        jnp.where(iota((n, n), 0) == iota((n, n), 1), row, jnp.zeros_like(row)),
        axis=1,
        keepdims=True,
    )


def row_of(col):
    n = col.shape[0]
    return jnp.sum(
        jnp.where(iota((n, n), 0) == iota((n, n), 1), col, jnp.zeros_like(col)),
        axis=0,
        keepdims=True,
    )


def side(a, b):
    return jnp.concatenate([a, b], axis=1)


def fixed(value):
    return jnp.floor(value * UNIT + 0.5).astype(I)


def stack(value, rows):
    return jnp.concatenate([value[:rows, 0:64], value[:rows, 64:128]], axis=0)


def fold(value):
    half = value.shape[0] // 2
    return side(value[:half, :], value[half:, :])


def kernel(*refs):
    hbm = refs[:15]
    result = refs[15]
    held_in = refs[16:30]
    (
        covers,
        linear,
        scores,
        nodes,
        lane_ids,
        group_ids,
        found_ids,
        row_ids,
        reply,
        replied,
        sums,
        parts,
        part_in,
        others,
        others_in,
        weight_in,
        other_in,
        parted,
        parted_in,
        whole,
        whole_others,
        local_sem,
        load_sem,
        send_sem,
        recv_sem,
    ) = refs[30:]
    cov = hbm[0]
    (
        weight,
        scale,
        z_lane,
        z_supplier,
        z_region,
        z_company,
        group_owner,
        group_local,
        group_len,
        event_bin,
        observed,
        lane_supplier,
        supplier_region,
        region_company,
    ) = held_in
    dp = lax.axis_index("dp")
    mp = lax.axis_index("mp")
    z = lax.div(dp, 8)
    yc = lax.rem(dp, 8)
    right = lax.rem(mp + 1, 4)
    left = lax.rem(mp + 3, 4)

    def at_z(step):
        return {"dp": lax.rem(z + step, 16) * 8 + yc, "mp": mp}

    def at_yc(step):
        return {"dp": z * 8 + lax.rem(yc + step, 8), "mp": mp}

    def at_x(index):
        return {"dp": dp, "mp": index}

    loads = []
    for k in range(14):
        copy = pltpu.make_async_copy(hbm[k + 1], held_in[k], load_sem.at[k])
        copy.start()
        loads.append(copy)

    barrier = pltpu.get_barrier_semaphore()
    partners = [at_z(step) for step in STEPS]
    partners += [at_yc(step) for step in range(1, 8)]
    partners += [at_x(right), at_x(left)]
    for device in partners:
        pl.semaphore_signal(
            barrier, inc=1, device_id=device, device_id_type=pl.DeviceIdType.MESH
        )

    own_copies = []
    for c in range(CHUNKS):
        rows = pl.ds(c * CH, CH)
        copy = pltpu.make_async_copy(cov.at[rows], covers.at[mp, rows], local_sem.at[c])
        copy.start()
        own_copies.append(copy)

    count = [0]
    started = []

    def send(src, dst, device):
        slot = count[0]
        count[0] = slot + 1
        copy = pltpu.make_async_remote_copy(
            src_ref=src,
            dst_ref=dst,
            send_sem=send_sem.at[slot],
            recv_sem=recv_sem.at[slot],
            device_id=device,
            device_id_type=pl.DeviceIdType.MESH,
        )
        copy.start()
        started.append(copy)
        return copy

    def arrive(copies):
        for copy in copies:
            copy.wait_recv()

    def along_z(buf):
        return [send(buf.at[z], buf.at[z], at_z(step)) for step in STEPS]

    def plane(buf):
        return [send(buf.at[yc], buf.at[yc], at_yc(step)) for step in range(1, 8)]

    def scatter(source, target):
        return [
            send(source.at[lax.rem(yc + step, 8)], target.at[yc], at_yc(step))
            for step in range(1, 8)
        ]

    direct = {}
    passed = {}

    def launch(c):
        rows = pl.ds(c * CH, CH)
        block = covers.at[mp, rows]
        direct[c] = [
            send(cov.at[rows], block, at_x(right)),
            send(cov.at[rows], block, at_x(left)),
        ]

    def forward(c):
        arrive(direct[c])
        first = covers.at[left, pl.ds(c * CH, HALF)]
        second = covers.at[right, pl.ds(c * CH + HALF, HALF)]
        passed[c] = [send(first, first, at_x(right)), send(second, second, at_x(left))]

    for copy in loads:
        copy.wait()
    own_owner = group_owner[...].astype(F)
    own_local = group_local[...].astype(F)
    nodes[z, 0:32, :] = fold(fixed(z_lane[...])).astype(S)
    nodes[z, 32:48, :] = fold(fixed(z_supplier[...])).astype(S)
    of_lane = lane_supplier[...]
    lane_ids[z] = side(of_lane >> 6, of_lane & 63).astype(F)
    group_ids[yc] = side(own_owner, own_local)
    pl.semaphore_wait(barrier, len(partners))

    lane_id_copies = along_z(lane_ids)
    group_id_copies = plane(group_ids)
    for c in range(CHUNKS):
        launch(c)
    node_copies = along_z(nodes)

    weight_rows = weight[...].astype(B)
    company_effect = scale[0:1, :] * z_company[...]
    companies = region_company[...]
    company_pick = pick(iota((64, 8), 1) == column(companies.astype(F)).astype(I))
    region_effect = scale[1:2, :] * z_region[...] + mm(
        company_pick, company_effect, precision=HIGHEST
    )
    lens = group_len[...].astype(F)
    spread = jnp.where(
        (iota((16, 64), 1) >> 2) == iota((16, 64), 0), lens, jnp.zeros_like(lens)
    )
    lanes_of = pick((iota((64, 128), 0) & 3) == (iota((64, 128), 1) >> 5), B)
    live_len = mm(spread.astype(B), lanes_of).astype(I)
    ends = jnp.where((iota((16, 128), 1) & 31) < live_len, event_bin[...], -1)
    flags = observed[...].astype(F)

    arrive(group_id_copies)
    ids = jnp.concatenate([group_ids[j] for j in range(8)], axis=0).astype(I)
    owners, locals_ = ids[:, 0:64], ids[:, 64:128]
    held = jnp.where((owners & 7) == yc, owners >> 3, -1)
    lane_key = jnp.where(held >= 0, held * 64 + locals_, -1)
    lane_columns = [
        column(lane_key[j : j + 1, :].astype(F)).astype(I) for j in range(8)
    ]

    def flat(rows):
        return jnp.concatenate([rows[j : j + 1, :] for j in range(8)], axis=1)

    owner_pick = pick(iota((16, 512), 0) == flat(held), B)
    local_pick = iota((64, 512), 0) == flat(locals_)
    forward(0)
    forward(1)
    forward(2)

    arrive(lane_id_copies)
    table = jnp.concatenate([lane_ids[k] for k in range(16)], axis=0).T.astype(B)
    of_owner = mm(table, owner_pick)
    of_owner = of_owner[0:64, :] * 64.0 + of_owner[64:128, :]
    found = jnp.sum(jnp.where(local_pick, of_owner, jnp.float32(0.0)), axis=0, keepdims=True)
    found = jnp.concatenate([found[:, j * 64 : j * 64 + 64] for j in range(8)], axis=0)
    found_ids[yc] = side(found, jnp.zeros((8, 64), F))
    found_copies = plane(found_ids)
    forward(3)
    forward(4)

    def digits(first, size):
        value = nodes[:, first : first + size, :].reshape(16 * size, 128).astype(I)
        high = (value + 64) >> 7
        low = value - (high << 7)
        return side(high.astype(F).astype(B), low.astype(F).astype(B))

    def chosen(row, upper, table):
        got = mm(pick(iota((64, table.shape[0]), 1) == row, B), table)
        got = got[:, 0:128] * 128.0 + got[:, 128:256]
        return jnp.where(upper, got[:, 64:128], got[:, 0:64])

    arrive(node_copies)
    lane_table = digits(0, 32)
    lane_parts = []
    for j in range(8):
        key = lane_columns[j]
        row = jnp.where(key >= 0, (key >> 6) * 32 + (key & 31), -1)
        lane_parts.append(chosen(row, (key & 32) > 0, lane_table))
    forward(5)

    arrive(found_copies)
    suppliers = found_ids[0]
    for j in range(1, 8):
        suppliers = suppliers + found_ids[j]
    suppliers = suppliers[:, 0:64]
    own_supplier = jnp.sum(
        jnp.where(iota((8, 64), 0) == yc, suppliers, jnp.float32(0.0)), axis=0, keepdims=True
    )
    row_ids[z] = side(own_supplier, own_owner * 64.0 + own_local)
    suppliers = suppliers.astype(I)
    sup_table = digits(32, 16)
    sup_key = jnp.where(((suppliers >> 5) & 7) == yc, suppliers, -1)
    for j in range(8):
        key = column(sup_key[j : j + 1, :].astype(F)).astype(I)
        row = jnp.where(key >= 0, (key >> 8) * 16 + (key & 15), -1)
        sup_part = chosen(row, (key & 16) > 0, sup_table)
        reply[j] = side(lane_parts[j], sup_part).astype(I).astype(S)
    replied[yc] = reply[yc]
    reply_copies = scatter(reply, replied)
    row_id_copies = along_z(row_ids)
    forward(6)

    own_sup_col = column(own_supplier).astype(I)
    sup_row = pick(iota((64, 32), 1) == (own_sup_col >> 7), B)
    region_table = mm(sup_row, supplier_region[...].astype(F).astype(B))
    group_region = jnp.sum(
        jnp.where(iota((64, 128), 1) == (own_sup_col & 127), region_table, jnp.float32(0.0)),
        axis=1,
        keepdims=True,
    )
    region_col = group_region.astype(I)
    region_row = row_of(group_region).astype(I)
    group_effect = mm(
        pick(iota((64, 64), 1) == region_col), region_effect, precision=HIGHEST
    )
    forward(7)

    def covered(first, last):
        return jnp.concatenate([covers[k, first * CH : last * CH, :] for k in range(4)], axis=1)

    def project(c):
        own_copies[c].wait()
        arrive(passed[c])
        linear[:, c * CH : (c + 1) * CH] = mm(weight_rows, covered(c, c + 1), 1, 1)

    for c in range(CHUNKS):
        project(c)

    arrive(reply_copies)
    got = replied[0].astype(I)
    for j in range(1, 8):
        got = got + replied[j].astype(I)
    got = got.astype(F) * (1.0 / UNIT)
    lane_latent, sup_latent = got[:, 0:64], got[:, 64:128]
    path = scale[2:3, :] * sup_latent + group_effect
    offset = (scale[3:4, :] * lane_latent + path).astype(B)
    offset = offset.astype(F).T.astype(B)

    bins = iota((64, 128), 0) + mp * 64

    def score_block(s):
        at = slice(s * 128, (s + 1) * 128)
        expand = pick(iota((64, 128), 0) == (iota((64, 128), 1) >> 5) + 4 * s, B)
        eta = linear[:, at] + mm(offset, expand)
        hazard = jax.nn.sigmoid(eta)
        end = ends[s : s + 1, :]
        score = jnp.where(
            bins < end,
            -hazard,
            jnp.where(bins == end, flags[s : s + 1, :] - hazard, jnp.float32(0.0)),
        )
        scores[:, at] = score.astype(B)

    product = None
    for first in range(0, CHUNKS, 2):
        for block in range(first * CH // 128, (first + 2) * CH // 128):
            score_block(block)
        part = mm(scores[:, first * CH : (first + 2) * CH], covered(first, first + 2))
        product = part if product is None else product + part
    for j in range(8):
        k, half = divmod(j, 2)
        parts[j] = product[half * 32 : half * 32 + 32, k * 128 : (k + 1) * 128]
    part_in[yc] = parts[yc]
    part_copies = scatter(parts, part_in)

    group_pick = pick(iota((64, 2048), 0) == (iota((64, 2048), 1) >> 5), B)
    group_sum = mm(group_pick, scores[...], 1, 1)
    sums[z] = fold(group_sum).astype(B)
    sum_copies = along_z(sums)

    by_region = fold(
        mm(pick(iota((64, 64), 0) == region_row), group_sum, precision=HIGHEST)
    )
    scale_part = side(
        jnp.sum(lane_latent * group_sum, axis=0, keepdims=True),
        jnp.sum(sup_latent * group_sum, axis=0, keepdims=True),
    )
    for j in range(4):
        others[j] = by_region[j * 8 : j * 8 + 8, :]
    others[4] = jnp.where(iota((8, 128), 0) == 0, scale_part, jnp.float32(0.0))
    for j in range(5, 8):
        others[j] = jnp.zeros((8, 128), F)
    others_in[yc] = others[yc]
    other_copies = scatter(others, others_in)

    arrive(row_id_copies)
    held_rows = jnp.concatenate([row_ids[k] for k in range(16)], axis=0).astype(I)

    def along(start):
        return jnp.concatenate(
            [held_rows[k : k + 1, start : start + 32] for k in range(16)], axis=1
        )

    sup_along = side(along(0), along(32)) - z * 256
    lane_along = side(along(64), along(96)) - z * 512
    lane_hit = pick(iota((512, 1024), 0) == lane_along, B)
    sup_hit = pick(iota((256, 1024), 0) == sup_along, B)

    def added(buf, many):
        total = buf[0].astype(F)
        for k in range(1, many):
            total = total + buf[k].astype(F)
        return total

    arrive(part_copies)
    weight_in[z] = added(part_in, 8).astype(B)
    weight_copies = along_z(weight_in)
    arrive(other_copies)
    other_in[z] = added(others_in, 8)
    other_copies = along_z(other_in)

    arrive(sum_copies)
    gathered = stack(sums[...].reshape(512, 128), 512)
    by_lane = mm(lane_hit, gathered)
    by_supplier = mm(sup_hit, gathered)
    for j in range(8):
        parted[j, 0:32, :] = fold(by_lane[j * 64 : j * 64 + 64, :])
        parted[j, 32:48, :] = fold(by_supplier[j * 32 : j * 32 + 32, :])
    parted_in[yc] = parted[yc]
    lane_copies = scatter(parted, parted_in)
    arrive(weight_copies)
    whole[yc] = added(weight_in, 16)
    whole_copies = plane(whole)
    arrive(other_copies)
    whole_others[yc] = added(other_in, 16)
    whole_other_copies = plane(whole_others)

    arrive(lane_copies)
    total = added(parted_in, 8)
    grad_lane = scale[3:4, :] * stack(total, 32) - z_lane[...]
    grad_supplier = scale[2:3, :] * stack(total[32:48, :], 16) - z_supplier[...]
    result[0:32, 640:768] = side(grad_supplier, jnp.zeros((32, 64), F))

    arrive(whole_copies)
    for j in range(8):
        k, half = divmod(j, 2)
        at = (slice(half * 32, half * 32 + 32), slice(k * 128, (k + 1) * 128))
        result[at] = whole[j] - weight[at]
    arrive(whole_other_copies)
    by_region = jnp.concatenate([whole_others[j] for j in range(4)], axis=0)
    region_total = stack(by_region, 32)
    scale_total = whole_others[4, 0:1, :]
    company_total = mm(
        pick(iota((8, 64), 0) == companies), region_total, precision=HIGHEST
    )
    grad_region = scale[1:2, :] * region_total - z_region[...]
    grad_company = scale[0:1, :] * company_total - z_company[...]
    result[:, 512:640] = side(grad_lane, grad_region)
    result[32:40, 640:768] = side(grad_company, jnp.zeros((8, 64), F))
    of_company = jnp.sum(z_company[...] * company_total, axis=0, keepdims=True)
    of_region = jnp.sum(z_region[...] * region_total, axis=0, keepdims=True)
    rank = iota((8, 64), 0)
    grad_scale = jnp.where(
        rank == 0,
        of_company,
        jnp.where(
            rank == 1,
            of_region,
            jnp.where(rank == 2, scale_total[:, 64:128], scale_total[:, 0:64]),
        ),
    )
    result[40:48, 640:768] = side(grad_scale, jnp.zeros((8, 64), F))
    result[48:64, 640:768] = jnp.zeros((16, 128), F)

    for copy in started:
        copy.wait_send()


def publish(
    result, grad_weight, grad_lane, grad_supplier, grad_region, grad_company, grad_scale
):
    grad_weight[...] = result[:, 0:512]
    pair = result[:, 512:640]
    grad_lane[...] = pair[:, 0:64]
    grad_region[...] = pair[:, 64:128]
    rest = result[:, 640:768]
    grad_supplier[...] = rest[0:32, 0:64]
    grad_company[...] = rest[32:40, 0:64]
    grad_scale[...] = rest[40:44, 0:64]


def per_device(
    covariates,
    weight,
    scale,
    z_lane,
    z_supplier,
    z_region,
    z_company,
    group_owner,
    group_local,
    group_len,
    event_bin,
    observed,
    lane_supplier,
    supplier_region,
    region_company,
):
    vmem = pl.BlockSpec(memory_space=pltpu.VMEM)
    hbm = pl.BlockSpec(memory_space=pltpu.HBM)
    operands = (
        covariates,
        weight.T,
        scale,
        z_lane,
        z_supplier,
        z_region,
        z_company,
        group_owner.reshape(1, 64),
        group_local.reshape(1, 64),
        group_len.reshape(1, 64),
        event_bin.reshape(16, 128),
        observed.reshape(16, 128),
        lane_supplier.reshape(1, 64),
        supplier_region.reshape(32, 128),
        region_company.reshape(1, 64),
    )
    shapes = ((64, 512), (64, 64), (32, 64), (64, 64), (8, 64), (4, 64))
    shapes = tuple(jax.ShapeDtypeStruct(shape, F) for shape in shapes)
    slots = 224
    result = pl.pallas_call(
        kernel,
        out_shape=pltpu.VMEM((64, 768), F),
        in_specs=[hbm] * 15,
        out_specs=vmem,
        scratch_shapes=[pltpu.VMEM(op.shape, op.dtype) for op in operands[1:]]
        + [
            pltpu.VMEM((4, ROWS, 128), B),
            pltpu.VMEM((64, ROWS), F),
            pltpu.VMEM((64, ROWS), B),
            pltpu.VMEM((16, 48, 128), S),
            pltpu.VMEM((16, 1, 128), F),
            pltpu.VMEM((8, 1, 128), F),
            pltpu.VMEM((8, 8, 128), F),
            pltpu.VMEM((16, 1, 128), F),
            pltpu.VMEM((8, 64, 128), S),
            pltpu.VMEM((8, 64, 128), S),
            pltpu.VMEM((16, 32, 128), B),
            pltpu.VMEM((8, 32, 128), F),
            pltpu.VMEM((8, 32, 128), F),
            pltpu.VMEM((8, 8, 128), F),
            pltpu.VMEM((8, 8, 128), F),
            pltpu.VMEM((16, 32, 128), B),
            pltpu.VMEM((16, 8, 128), F),
            pltpu.VMEM((8, 48, 128), F),
            pltpu.VMEM((8, 48, 128), F),
            pltpu.VMEM((8, 32, 128), F),
            pltpu.VMEM((8, 8, 128), F),
            pltpu.SemaphoreType.DMA((CHUNKS,)),
            pltpu.SemaphoreType.DMA((14,)),
            pltpu.SemaphoreType.DMA((slots,)),
            pltpu.SemaphoreType.DMA((slots,)),
        ],
        compiler_params=pltpu.CompilerParams(
            collective_id=0, has_side_effects=True, vmem_limit_bytes=VMEM_BYTES
        ),
        name="hazard_gradient",
    )(*operands)
    results = pl.pallas_call(
        publish,
        out_shape=shapes,
        in_specs=[vmem],
        out_specs=tuple(pl.BlockSpec(shape.shape, lambda: (0, 0)) for shape in shapes),
        name="publish",
    )(result)
    return (results[0].T,) + tuple(results[1:])


def solution(mesh):
    in_specs = (
        P("dp", "mp"),
        P(None, "mp"),
        P(None, "mp"),
        P("dp", "mp"),
        P("dp", "mp"),
        P(None, "mp"),
        P(None, "mp"),
        P("dp", None),
        P("dp"),
        P("dp"),
        P("dp"),
        P("dp"),
        P("dp"),
        P(),
        P(),
    )
    out_specs = (
        P(None, "mp"),
        P("dp", "mp"),
        P("dp", "mp"),
        P(None, "mp"),
        P(None, "mp"),
        P(None, "mp"),
    )
    return jax.shard_map(
        per_device, mesh=mesh, in_specs=in_specs, out_specs=out_specs, check_vma=False
    )
```

time: 737 us -> 67.5 us (0.09)
  waiting for transfers between devices: 382 us -> 0 us
  blocking collectives: 247 us -> 0 us
  Pallas kernels: 0 us -> 66.1 us
  starting transfers between devices: 49.5 us -> 0 us
  matrix products: 16.3 us -> 0 us
  local copies, waits for them, and re-layouts: 15 us -> 0.66 us
  between operations: 14 us -> 0.65 us
  other arithmetic: 11.8 us -> 0 us
    all_gather x3 -> x0, waiting for transfers between devices: 262 us -> none  [the longest x1 122 us: per_device(): lax.all_gather(z_supplier, 'dp', axis=0, tiled=True)]
    psum x1 -> x0, blocking collectives: 247 us -> none  [per_device(): lax.psum((supplier_part, weight_part, scale_part), 'dp')]
    psum x1 -> x0, waiting for transfers between devices: 93.3 us -> none  [per_device(): lax.psum((supplier_part, weight_part, scale_part), 'dp')]
    pallas_call x0 -> x2, Pallas kernels: none -> 66.1 us  [the longest x1 64.4 us: per_device(): pl.pallas_call(kernel, out_shape=pltpu.VMEM((64, 768), F), in_specs=[hbm]...]
    all_to_all x3 -> x0, starting transfers between devices: 49.3 us -> none  [the longest x1 20.7 us: per_device(): lax.all_to_all(request, 'dp', split_axis=0, concat_axis=0, tiled=True)]
    all_to_all x3 -> x0, waiting for transfers between devices: 25.3 us -> none  [the longest x1 12.8 us: per_device(): lax.all_to_all(request, 'dp', split_axis=0, concat_axis=0, tiled=True)]
    dot_general x8 -> x0, matrix products: 16.3 us -> none  [the longest x2 6.47 us: total_rows(): lax.dot_general(picks, values, (((0,), (0,)), ((), ())), precision=HIGHEST)]
  transfers between devices with their start and end apart: 7 -> 0, of which waited for: 6 -> 0; matrix products, arithmetic and copies ran while one was open for 2% -> 0% of each run, Pallas kernels for 0% -> 0%
where the time goes in v2:
time: 67.5 us; the launch traced here: 67.4 us
  Pallas kernels  66.1 us (98%)
    pallas_call x1, Pallas kernels, per_device(): pl.pallas_call(kernel, out_shape=pltpu.VMEM((64, 768), F), in_specs=[hbm]...  64.4 us
    pallas_call x1, Pallas kernels, per_device(): pl.pallas_call(publish, out_shape=shapes, in_specs=[vmem], out_specs=tupl...  1.62 us

profile of v2, /device:TPU:1, one launch (start us, length us, event | category | flops | bytes accessed | tf_op | source)
XLA Modules:
  0.0 67.4 jit_solution(14076221355734497029)
XLA Ops:
  0.6 64.4 %hazard_gradient.1.result = f32[64,768]{1,0:T(8,128)S(1)} custom-call(bf16[2048,128]{1,0:T(8,128)(2,1)} %refs_0_.1, f32[64,512]{1,0:T(8,128)} %bitcast.10, f32[4,64]{1,0:T(4,128)} %refs_2_.1, f32[64,64]{1,0:T(8,128)} %refs_3_.1, f32[32,64]{1,0:T(8,128)} %refs_4_.1, f32[64,64]{1,0:T(8,128)} %refs_5_.1, f32[8,64]{1,0:T(8,128)} %refs_6_.1, s32[1,64]{1,0:T(1,128)} %bitcast.14, ...), custom_call_target="tpu_custom_call" | custom-call | tf_op jit(solution)/shard_map/hazard_gradient/pallas_call | solution.py:530
  65.1 0.0 copy-start
  65.1 0.7 copy-done
  65.8 1.6 %publish.1 = (f32[64,512]{1,0:T(8,128)}, f32[64,64]{1,0:T(8,128)}, f32[32,64]{1,0:T(8,128)}, f32[64,64]{1,0:T(8,128)}, f32[8,64]{1,0:T(8,128)}, /*index=5*/f32[4,64]{1,0:T(4,128)}) custom-call(f32[64,768]{1,0:T(8,128)} %copy-done), custom_call_target="tpu_custom_call" | custom-call | tf_op jit(solution)/shard_map/publish/pallas_call | solution.py:568
Async XLA Ops:
  65.1 0.7 copy-start

commit v3 on v2

--- a/solution.py
+++ b/solution.py
@@ -83,17 +83,17 @@
         row_ids,
         reply,
         replied,
+        sup_reply,
+        sup_replied,
         sums,
         parts,
         part_in,
-        others,
-        others_in,
         weight_in,
-        other_in,
+        scale_rows,
+        scale_in,
         parted,
         parted_in,
         whole,
-        whole_others,
         local_sem,
         load_sem,
         send_sem,
@@ -132,12 +132,6 @@
     def at_x(index):
         return {"dp": dp, "mp": index}
 
-    loads = []
-    for k in range(14):
-        copy = pltpu.make_async_copy(hbm[k + 1], held_in[k], load_sem.at[k])
-        copy.start()
-        loads.append(copy)
-
     barrier = pltpu.get_barrier_semaphore()
     partners = [at_z(step) for step in STEPS]
     partners += [at_yc(step) for step in range(1, 8)]
@@ -146,6 +140,12 @@
         pl.semaphore_signal(
             barrier, inc=1, device_id=device, device_id_type=pl.DeviceIdType.MESH
         )
+
+    loads = []
+    for k in range(14):
+        copy = pltpu.make_async_copy(hbm[k + 1], held_in[k], load_sem.at[k])
+        copy.start()
+        loads.append(copy)
 
     own_copies = []
     for c in range(CHUNKS):
@@ -216,11 +216,15 @@
     group_ids[yc] = side(own_owner, own_local)
     pl.semaphore_wait(barrier, len(partners))
 
+    for c in range(2):
+        launch(c)
     lane_id_copies = along_z(lane_ids)
     group_id_copies = plane(group_ids)
-    for c in range(CHUNKS):
+    for c in range(2, 4):
         launch(c)
     node_copies = along_z(nodes)
+    for c in range(4, CHUNKS):
+        launch(c)
 
     weight_rows = weight[...].astype(B)
     company_effect = scale[0:1, :] * z_company[...]
@@ -280,11 +284,12 @@
 
     arrive(node_copies)
     lane_table = digits(0, 32)
-    lane_parts = []
     for j in range(8):
         key = lane_columns[j]
         row = jnp.where(key >= 0, (key >> 6) * 32 + (key & 31), -1)
-        lane_parts.append(chosen(row, (key & 32) > 0, lane_table))
+        reply[j] = fold(chosen(row, (key & 32) > 0, lane_table)).astype(I).astype(S)
+    replied[yc] = reply[yc]
+    reply_copies = scatter(reply, replied)
     forward(5)
 
     arrive(found_copies)
@@ -295,18 +300,15 @@
     own_supplier = jnp.sum(
         jnp.where(iota((8, 64), 0) == yc, suppliers, jnp.float32(0.0)), axis=0, keepdims=True
     )
-    row_ids[z] = side(own_supplier, own_owner * 64.0 + own_local)
     suppliers = suppliers.astype(I)
     sup_table = digits(32, 16)
     sup_key = jnp.where(((suppliers >> 5) & 7) == yc, suppliers, -1)
     for j in range(8):
         key = column(sup_key[j : j + 1, :].astype(F)).astype(I)
         row = jnp.where(key >= 0, (key >> 8) * 16 + (key & 15), -1)
-        sup_part = chosen(row, (key & 16) > 0, sup_table)
-        reply[j] = side(lane_parts[j], sup_part).astype(I).astype(S)
-    replied[yc] = reply[yc]
-    reply_copies = scatter(reply, replied)
-    row_id_copies = along_z(row_ids)
+        sup_reply[j] = fold(chosen(row, (key & 16) > 0, sup_table)).astype(I).astype(S)
+    sup_replied[yc] = sup_reply[yc]
+    reply_copies += scatter(sup_reply, sup_replied)
     forward(6)
 
     own_sup_col = column(own_supplier).astype(I)
@@ -318,7 +320,10 @@
         keepdims=True,
     )
     region_col = group_region.astype(I)
-    region_row = row_of(group_region).astype(I)
+    row_ids[z] = side(
+        own_supplier * 64.0 + row_of(group_region), own_owner * 64.0 + own_local
+    )
+    row_id_copies = along_z(row_ids)
     group_effect = mm(
         pick(iota((64, 64), 1) == region_col), region_effect, precision=HIGHEST
     )
@@ -336,11 +341,14 @@
         project(c)
 
     arrive(reply_copies)
-    got = replied[0].astype(I)
-    for j in range(1, 8):
-        got = got + replied[j].astype(I)
-    got = got.astype(F) * (1.0 / UNIT)
-    lane_latent, sup_latent = got[:, 0:64], got[:, 64:128]
+
+    def latent(buf):
+        got = buf[0].astype(I)
+        for j in range(1, 8):
+            got = got + buf[j].astype(I)
+        return stack(got.astype(F) * (1.0 / UNIT), 32)
+
+    lane_latent, sup_latent = latent(replied), latent(sup_replied)
     path = scale[2:3, :] * sup_latent + group_effect
     offset = (scale[3:4, :] * lane_latent + path).astype(B)
     offset = offset.astype(F).T.astype(B)
@@ -368,7 +376,8 @@
         product = part if product is None else product + part
     for j in range(8):
         k, half = divmod(j, 2)
-        parts[j] = product[half * 32 : half * 32 + 32, k * 128 : (k + 1) * 128]
+        block = product[half * 32 : half * 32 + 32, k * 128 : (k + 1) * 128]
+        parts[j] = block.astype(B)
     part_in[yc] = parts[yc]
     part_copies = scatter(parts, part_in)
 
@@ -377,20 +386,11 @@
     sums[z] = fold(group_sum).astype(B)
     sum_copies = along_z(sums)
 
-    by_region = fold(
-        mm(pick(iota((64, 64), 0) == region_row), group_sum, precision=HIGHEST)
-    )
-    scale_part = side(
+    scale_rows[z] = side(
         jnp.sum(lane_latent * group_sum, axis=0, keepdims=True),
         jnp.sum(sup_latent * group_sum, axis=0, keepdims=True),
     )
-    for j in range(4):
-        others[j] = by_region[j * 8 : j * 8 + 8, :]
-    others[4] = jnp.where(iota((8, 128), 0) == 0, scale_part, jnp.float32(0.0))
-    for j in range(5, 8):
-        others[j] = jnp.zeros((8, 128), F)
-    others_in[yc] = others[yc]
-    other_copies = scatter(others, others_in)
+    scale_copies = along_z(scale_rows)
 
     arrive(row_id_copies)
     held_rows = jnp.concatenate([row_ids[k] for k in range(16)], axis=0).astype(I)
@@ -400,10 +400,13 @@
             [held_rows[k : k + 1, start : start + 32] for k in range(16)], axis=1
         )
 
-    sup_along = side(along(0), along(32)) - z * 256
+    sup_along = side(along(0), along(32))
+    region_along = sup_along & 63
+    sup_along = (sup_along >> 6) - z * 256
     lane_along = side(along(64), along(96)) - z * 512
     lane_hit = pick(iota((512, 1024), 0) == lane_along, B)
     sup_hit = pick(iota((256, 1024), 0) == sup_along, B)
+    region_hit = pick(iota((64, 1024), 0) == region_along, B)
 
     def added(buf, many):
         total = buf[0].astype(F)
@@ -414,41 +417,34 @@
     arrive(part_copies)
     weight_in[z] = added(part_in, 8).astype(B)
     weight_copies = along_z(weight_in)
-    arrive(other_copies)
-    other_in[z] = added(others_in, 8)
-    other_copies = along_z(other_in)
 
     arrive(sum_copies)
     gathered = stack(sums[...].reshape(512, 128), 512)
     by_lane = mm(lane_hit, gathered)
     by_supplier = mm(sup_hit, gathered)
+    by_region = fold(mm(region_hit, gathered)).astype(B)
     for j in range(8):
-        parted[j, 0:32, :] = fold(by_lane[j * 64 : j * 64 + 64, :])
-        parted[j, 32:48, :] = fold(by_supplier[j * 32 : j * 32 + 32, :])
+        parted[j, 0:32, :] = fold(by_lane[j * 64 : j * 64 + 64, :]).astype(B)
+        parted[j, 32:48, :] = fold(by_supplier[j * 32 : j * 32 + 32, :]).astype(B)
+        parted[j, 48:80, :] = by_region
     parted_in[yc] = parted[yc]
     lane_copies = scatter(parted, parted_in)
+    arrive(scale_copies)
+    scale_in[yc] = added(scale_rows, 16)
+    scale_copies = plane(scale_in)
+
     arrive(weight_copies)
     whole[yc] = added(weight_in, 16)
     whole_copies = plane(whole)
-    arrive(other_copies)
-    whole_others[yc] = added(other_in, 16)
-    whole_other_copies = plane(whole_others)
 
     arrive(lane_copies)
     total = added(parted_in, 8)
     grad_lane = scale[3:4, :] * stack(total, 32) - z_lane[...]
     grad_supplier = scale[2:3, :] * stack(total[32:48, :], 16) - z_supplier[...]
+    region_total = stack(total[48:80, :], 32)
     result[0:32, 640:768] = side(grad_supplier, jnp.zeros((32, 64), F))
-
-    arrive(whole_copies)
-    for j in range(8):
-        k, half = divmod(j, 2)
-        at = (slice(half * 32, half * 32 + 32), slice(k * 128, (k + 1) * 128))
-        result[at] = whole[j] - weight[at]
-    arrive(whole_other_copies)
-    by_region = jnp.concatenate([whole_others[j] for j in range(4)], axis=0)
-    region_total = stack(by_region, 32)
-    scale_total = whole_others[4, 0:1, :]
+    arrive(scale_copies)
+    scale_total = added(scale_in, 8)
     company_total = mm(
         pick(iota((8, 64), 0) == companies), region_total, precision=HIGHEST
     )
@@ -470,6 +466,12 @@
     )
     result[40:48, 640:768] = side(grad_scale, jnp.zeros((8, 64), F))
     result[48:64, 640:768] = jnp.zeros((16, 128), F)
+
+    arrive(whole_copies)
+    for j in range(8):
+        k, half = divmod(j, 2)
+        at = (slice(half * 32, half * 32 + 32), slice(k * 128, (k + 1) * 128))
+        result[at] = whole[j] - weight[at]
 
     for copy in started:
         copy.wait_send()
@@ -542,19 +544,19 @@
             pltpu.VMEM((8, 1, 128), F),
             pltpu.VMEM((8, 8, 128), F),
             pltpu.VMEM((16, 1, 128), F),
-            pltpu.VMEM((8, 64, 128), S),
-            pltpu.VMEM((8, 64, 128), S),
+            pltpu.VMEM((8, 32, 128), S),
+            pltpu.VMEM((8, 32, 128), S),
+            pltpu.VMEM((8, 32, 128), S),
+            pltpu.VMEM((8, 32, 128), S),
             pltpu.VMEM((16, 32, 128), B),
+            pltpu.VMEM((8, 32, 128), B),
+            pltpu.VMEM((8, 32, 128), B),
+            pltpu.VMEM((16, 32, 128), B),
+            pltpu.VMEM((16, 1, 128), F),
+            pltpu.VMEM((8, 1, 128), F),
+            pltpu.VMEM((8, 80, 128), B),
+            pltpu.VMEM((8, 80, 128), B),
             pltpu.VMEM((8, 32, 128), F),
-            pltpu.VMEM((8, 32, 128), F),
-            pltpu.VMEM((8, 8, 128), F),
-            pltpu.VMEM((8, 8, 128), F),
-            pltpu.VMEM((16, 32, 128), B),
-            pltpu.VMEM((16, 8, 128), F),
-            pltpu.VMEM((8, 48, 128), F),
-            pltpu.VMEM((8, 48, 128), F),
-            pltpu.VMEM((8, 32, 128), F),
-            pltpu.VMEM((8, 8, 128), F),
             pltpu.SemaphoreType.DMA((CHUNKS,)),
             pltpu.SemaphoreType.DMA((14,)),
             pltpu.SemaphoreType.DMA((slots,)),

time: 67.5 us -> 63.1 us (0.935)
  Pallas kernels: 66.1 us -> 61.6 us
    pallas_call x1, Pallas kernels: 64.4 us -> 59.9 us  [per_device(): pl.pallas_call(kernel, out_shape=pltpu.VMEM((64, 768), F), in_specs=[hbm]...]
where the time goes in v3:
time: 63.1 us; the launch traced here: 62.9 us
  Pallas kernels  61.6 us (98%)
  local copies, waits for them, and re-layouts  0.66 us (1%)
  between operations  0.65 us (1%)
    pallas_call x1, Pallas kernels, per_device(): pl.pallas_call(kernel, out_shape=pltpu.VMEM((64, 768), F), in_specs=[hbm]...  59.9 us
    pallas_call x1, Pallas kernels, per_device(): pl.pallas_call(publish, out_shape=shapes, in_specs=[vmem], out_specs=tupl...  1.62 us

profile of v3, /device:TPU:1, one launch (start us, length us, event | category | flops | bytes accessed | tf_op | source)
XLA Modules:
  0.0 62.9 jit_solution(9863753751006470263)
XLA Ops:
  0.6 59.9 %hazard_gradient.1.result = f32[64,768]{1,0:T(8,128)S(1)} custom-call(bf16[2048,128]{1,0:T(8,128)(2,1)} %refs_0_.1, f32[64,512]{1,0:T(8,128)} %bitcast.10, f32[4,64]{1,0:T(4,128)} %refs_2_.1, f32[64,64]{1,0:T(8,128)} %refs_3_.1, f32[32,64]{1,0:T(8,128)} %refs_4_.1, f32[64,64]{1,0:T(8,128)} %refs_5_.1, f32[8,64]{1,0:T(8,128)} %refs_6_.1, s32[1,64]{1,0:T(1,128)} %bitcast.14, ...), custom_call_target="tpu_custom_call" | custom-call | tf_op jit(solution)/shard_map/hazard_gradient/pallas_call | solution.py:532
  60.6 0.0 copy-start
  60.6 0.7 %copy-done = f32[64,768]{1,0:T(8,128)} copy-done((f32[64,768]{1,0:T(8,128)}, f32[64,768]{1,0:T(8,128)S(1)}, u32[]{:S(2)}) %copy-start) | copy-done | bytes 196632
  61.3 1.6 %publish.1 = (f32[64,512]{1,0:T(8,128)}, f32[64,64]{1,0:T(8,128)}, f32[32,64]{1,0:T(8,128)}, f32[64,64]{1,0:T(8,128)}, f32[8,64]{1,0:T(8,128)}, /*index=5*/f32[4,64]{1,0:T(4,128)}) custom-call(f32[64,768]{1,0:T(8,128)} %copy-done), custom_call_target="tpu_custom_call" | custom-call | tf_op jit(solution)/shard_map/publish/pallas_call | solution.py:570
Async XLA Ops:
  60.6 0.7 %copy-start = (f32[64,768]{1,0:T(8,128)}, f32[64,768]{1,0:T(8,128)S(1)}, u32[]{:S(2)}) copy-start(f32[64,768]{1,0:T(8,128)S(1)} %hazard_gradient.1.result) | copy-start | bytes 589828

commit v4 on v3

--- a/solution.py
+++ b/solution.py
@@ -172,6 +172,10 @@
         started.append(copy)
         return copy
 
+    def settle(first, last):
+        for copy in started[first:last]:
+            copy.wait_send()
+
     def arrive(copies):
         for copy in copies:
             copy.wait_recv()
@@ -368,10 +372,15 @@
         )
         scores[:, at] = score.astype(B)
 
+    for block in range(16):
+        score_block(block)
+    group_pick = pick(iota((64, 2048), 0) == (iota((64, 2048), 1) >> 5), B)
+    group_sum = mm(group_pick, scores[...], 1, 1)
+    sums[z] = fold(group_sum).astype(B)
+    sum_copies = along_z(sums)
+
     product = None
     for first in range(0, CHUNKS, 2):
-        for block in range(first * CH // 128, (first + 2) * CH // 128):
-            score_block(block)
         part = mm(scores[:, first * CH : (first + 2) * CH], covered(first, first + 2))
         product = part if product is None else product + part
     for j in range(8):
@@ -379,12 +388,8 @@
         block = product[half * 32 : half * 32 + 32, k * 128 : (k + 1) * 128]
         parts[j] = block.astype(B)
     part_in[yc] = parts[yc]
+    before_parts = count[0]
     part_copies = scatter(parts, part_in)
-
-    group_pick = pick(iota((64, 2048), 0) == (iota((64, 2048), 1) >> 5), B)
-    group_sum = mm(group_pick, scores[...], 1, 1)
-    sums[z] = fold(group_sum).astype(B)
-    sum_copies = along_z(sums)
 
     scale_rows[z] = side(
         jnp.sum(lane_latent * group_sum, axis=0, keepdims=True),
@@ -433,8 +438,10 @@
     scale_in[yc] = added(scale_rows, 16)
     scale_copies = plane(scale_in)
 
+    settle(0, before_parts)
     arrive(weight_copies)
     whole[yc] = added(weight_in, 16)
+    before_whole = count[0]
     whole_copies = plane(whole)
 
     arrive(lane_copies)
@@ -467,14 +474,14 @@
     result[40:48, 640:768] = side(grad_scale, jnp.zeros((8, 64), F))
     result[48:64, 640:768] = jnp.zeros((16, 128), F)
 
+    settle(before_parts, before_whole)
     arrive(whole_copies)
     for j in range(8):
         k, half = divmod(j, 2)
         at = (slice(half * 32, half * 32 + 32), slice(k * 128, (k + 1) * 128))
         result[at] = whole[j] - weight[at]
 
-    for copy in started:
-        copy.wait_send()
+    settle(before_whole, count[0])
 
 
 def publish(
@@ -573,7 +580,7 @@
         in_specs=[vmem],
         out_specs=tuple(pl.BlockSpec(shape.shape, lambda: (0, 0)) for shape in shapes),
         name="publish",
-    )(result)
+    )(pltpu.with_memory_space_constraint(result, pltpu.VMEM))
     return (results[0].T,) + tuple(results[1:])
 
 

time: 63.1 us -> 60.7 us (0.962)
  Pallas kernels: 61.6 us -> 59.9 us
  local copies, waits for them, and re-layouts: 0.66 us -> 0 us
    pallas_call x1, Pallas kernels: 1.62 us -> 0.7 us  [per_device(): pl.pallas_call(publish, out_shape=shapes, in_specs=[vmem], out_specs=tupl...]
    pallas_call x1, Pallas kernels: 59.9 us -> 59.2 us  [per_device(): pl.pallas_call(kernel, out_shape=pltpu.VMEM((64, 768), F), in_specs=[hbm]...]
    unnamed x2 -> x0, local copies, waits for them, and re-layouts: 0.66 us -> none
where the time goes in v4:
time: 60.7 us; the launch traced here: 60.5 us
  Pallas kernels  59.9 us (99%)
  between operations  0.65 us (1%)
    pallas_call x1, Pallas kernels, per_device(): pl.pallas_call(kernel, out_shape=pltpu.VMEM((64, 768), F), in_specs=[hbm]...  59.2 us

profile of v4, /device:TPU:1, one launch (start us, length us, event | category | flops | bytes accessed | tf_op | source)
XLA Modules:
  0.0 60.5 jit_solution(10262814788102078886)
XLA Ops:
  0.6 59.2 %hazard_gradient.1.result = f32[64,768]{1,0:T(8,128)S(1)} custom-call(bf16[2048,128]{1,0:T(8,128)(2,1)} %refs_0_.1, f32[64,512]{1,0:T(8,128)} %bitcast.10, f32[4,64]{1,0:T(4,128)} %refs_2_.1, f32[64,64]{1,0:T(8,128)} %refs_3_.1, f32[32,64]{1,0:T(8,128)} %refs_4_.1, f32[64,64]{1,0:T(8,128)} %refs_5_.1, f32[8,64]{1,0:T(8,128)} %refs_6_.1, s32[1,64]{1,0:T(1,128)} %bitcast.14, ...), custom_call_target="tpu_custom_call" | custom-call | tf_op jit(solution)/shard_map/hazard_gradient/pallas_call | solution.py:539
  59.8 0.7 %publish.1 = (f32[64,512]{1,0:T(8,128)}, f32[64,64]{1,0:T(8,128)}, f32[32,64]{1,0:T(8,128)}, f32[64,64]{1,0:T(8,128)}, f32[8,64]{1,0:T(8,128)}, /*index=5*/f32[4,64]{1,0:T(4,128)}) custom-call(f32[64,768]{1,0:T(8,128)S(1)} %hazard_gradient.1.result), custom_call_target="tpu_custom_call" | custom-call | tf_op jit(solution)/shard_map/publish/pallas_call | solution.py:577

commit v5 on v4

--- a/solution.py
+++ b/solution.py
@@ -341,7 +341,7 @@
         arrive(passed[c])
         linear[:, c * CH : (c + 1) * CH] = mm(weight_rows, covered(c, c + 1), 1, 1)
 
-    for c in range(CHUNKS):
+    for c in range(6):
         project(c)
 
     arrive(reply_copies)
@@ -357,6 +357,8 @@
     offset = (scale[3:4, :] * lane_latent + path).astype(B)
     offset = offset.astype(F).T.astype(B)
 
+    for c in range(6, CHUNKS):
+        project(c)
     bins = iota((64, 128), 0) + mp * 64
 
     def score_block(s):
@@ -397,6 +399,16 @@
     )
     scale_copies = along_z(scale_rows)
 
+    def added(buf, many):
+        total = buf[0].astype(F)
+        for k in range(1, many):
+            total = total + buf[k].astype(F)
+        return total
+
+    arrive(part_copies)
+    weight_in[z] = added(part_in, 8).astype(B)
+    weight_copies = along_z(weight_in)
+
     arrive(row_id_copies)
     held_rows = jnp.concatenate([row_ids[k] for k in range(16)], axis=0).astype(I)
 
@@ -412,16 +424,6 @@
     lane_hit = pick(iota((512, 1024), 0) == lane_along, B)
     sup_hit = pick(iota((256, 1024), 0) == sup_along, B)
     region_hit = pick(iota((64, 1024), 0) == region_along, B)
-
-    def added(buf, many):
-        total = buf[0].astype(F)
-        for k in range(1, many):
-            total = total + buf[k].astype(F)
-        return total
-
-    arrive(part_copies)
-    weight_in[z] = added(part_in, 8).astype(B)
-    weight_copies = along_z(weight_in)
 
     arrive(sum_copies)
     gathered = stack(sums[...].reshape(512, 128), 512)

time: 60.7 us -> 60.3 us (level)
  no operation moved by 1% of the time
where the time goes in v5:
time: 60.3 us; the launch traced here: 60.1 us
  Pallas kernels  59.5 us (99%)
  between operations  0.65 us (1%)
    pallas_call x1, Pallas kernels, per_device(): pl.pallas_call(kernel, out_shape=pltpu.VMEM((64, 768), F), in_specs=[hbm]...  58.8 us

profile of v5, /device:TPU:1, one launch (start us, length us, event | category | flops | bytes accessed | tf_op | source)
XLA Modules:
  0.0 60.1 jit_solution(14529698540882928037)
XLA Ops:
  0.6 58.8 %hazard_gradient.1.result = f32[64,768]{1,0:T(8,128)S(1)} custom-call(bf16[2048,128]{1,0:T(8,128)(2,1)} %refs_0_.1, f32[64,512]{1,0:T(8,128)} %bitcast.10, f32[4,64]{1,0:T(4,128)} %refs_2_.1, f32[64,64]{1,0:T(8,128)} %refs_3_.1, f32[32,64]{1,0:T(8,128)} %refs_4_.1, f32[64,64]{1,0:T(8,128)} %refs_5_.1, f32[8,64]{1,0:T(8,128)} %refs_6_.1, s32[1,64]{1,0:T(1,128)} %bitcast.14, ...), custom_call_target="tpu_custom_call" | custom-call | tf_op jit(solution)/shard_map/hazard_gradient/pallas_call | solution.py:541
  59.4 0.7 %publish.1 = (f32[64,512]{1,0:T(8,128)}, f32[64,64]{1,0:T(8,128)}, f32[32,64]{1,0:T(8,128)}, f32[64,64]{1,0:T(8,128)}, f32[8,64]{1,0:T(8,128)}, /*index=5*/f32[4,64]{1,0:T(4,128)}) custom-call(f32[64,768]{1,0:T(8,128)S(1)} %hazard_gradient.1.result), custom_call_target="tpu_custom_call" | custom-call | tf_op jit(solution)/shard_map/publish/pallas_call | solution.py:579
